TPU v7x, 256 devices: a whole 4x4x8 slice. The times are simulated.
256 devices in a mesh: ep: 64 (over y, x_lo, z), dp: 4 (over x_hi, core).
Axes of the slice: x: 4 (x_hi: 2, x_lo: 2; x = x_hi * 2 + x_lo), y: 4, z: 8, core: 2. Of those that a mesh axis runs over, the one named last changes fastest.
Arguments:
- tokens: bfloat16 [8192, 7168], P('ep', 'dp'), may hold values from -6 to 6
- cotangent: bfloat16 [8192, 7168], P('ep', 'dp'), may hold values from -0.29882812 to 0.29882812
- gate_prob: bfloat16 [8192, 2], P('ep'), may hold values from 0.099609375 to 1
- expert_ids: int32 [8192, 2], P('ep'), may hold values from 0 to 31, all different within a row; in each aligned block of 128 rows (0 to 127, 128 to 255, ...) at most 10 rows name the same one
- w_up: bfloat16 [64, 7168, 512], P('ep', 'dp'), may hold values from -0.0625 to 0.0625
- w_down: bfloat16 [64, 512, 7168], P('ep', None, 'dp'), may hold values from -0.1875 to 0.1875
Outputs:
- grad_tokens: bfloat16 [8192, 7168], P('ep', 'dp')
- grad_gate: float32 [8192, 2], P('ep')
- grad_up: bfloat16 [64, 7168, 512], P('ep', 'dp')
- grad_down: bfloat16 [64, 512, 7168], P('ep', None, 'dp')
Inputs may be any that keep to these rules, and one draw needn't show every extreme that they name: `expert_ids`: the 2 experts of one token differ. Among the routes of the tokens of one index of ep (aligned blocks of 128 tokens), no expert is named more than 10 times, a bound that some block reaches.
All inputs are finite; a program needn't handle non-finite values.
Results may differ from a plain program's by a relative error of at most 0.012.
Values may be sent and summed in bfloat16 or wider, within the bound.
A program may use at most 128 MiB of HBM per device.

v0:
```python
import jax
import jax.numpy as jnp
from jax import lax
from jax.sharding import PartitionSpec as P


def passed_along(value, axis, steps):
    count = lax.axis_size(axis)
    pairs = [(source, (source + steps) % count) for source in range(count)]
    return lax.ppermute(value, axis, pairs)


def silu_slope(preact):
    sigmoid_val = jax.nn.sigmoid(preact)
    return sigmoid_val * (1.0 + preact * (1.0 - sigmoid_val))


def doubled(send_buffer, expert_count, capacity):
    tail_dims = send_buffer.shape[1:]
    reshaped = send_buffer.reshape((expert_count, 1, 2 * capacity) + tail_dims)
    spread_out = jnp.broadcast_to(reshaped, (expert_count, 2, 2 * capacity) + tail_dims)
    return spread_out.reshape((2 * expert_count, 2 * capacity) + tail_dims)


def on_device(tokens, cotangent, gate_prob, expert_ids, w_up, w_down):
    device_count = lax.axis_size("ep")
    expert_count = device_count // 2
    tok_rows, feature_cols = tokens.shape
    route_count = expert_ids.shape[1]
    capacity = 2 * (5 * tok_rows * route_count // (4 * device_count))
    source_device = lax.axis_index("ep")
    copy_up, copy_down = passed_along((w_up, w_down), "ep", device_count // 2)
    flat_ids = expert_ids.reshape(-1)
    to_replica = jnp.full(flat_ids.shape, source_device >= expert_count)
    copy_group = to_replica.astype(jnp.int32)
    target_pair = jnp.where(to_replica, (flat_ids + expert_count // 2) % expert_count, flat_ids)
    one_hot = (flat_ids[:, None] == jnp.arange(expert_count, dtype=jnp.int32)[None, :]).astype(
        jnp.int32
    )
    slot_rank = jnp.sum((jnp.cumsum(one_hot, axis=0) - one_hot) * one_hot, axis=1)
    slot_index = (target_pair * 2 + copy_group) * capacity + slot_rank
    token_row = jnp.arange(tok_rows * route_count, dtype=jnp.int32) // route_count
    total_slots = expert_count * 2 * capacity
    send_x = (
        jnp.zeros((total_slots, feature_cols), jnp.bfloat16).at[slot_index].set(tokens[token_row])
    )
    send_dy = (
        jnp.zeros((total_slots, feature_cols), jnp.bfloat16)
        .at[slot_index]
        .set(cotangent[token_row])
    )
    send_gate = jnp.zeros((total_slots,), jnp.bfloat16).at[slot_index].set(gate_prob.reshape(-1))
    got_x, got_dy, got_gate = (
        lax.all_to_all(
            doubled(send_x, expert_count, capacity), "ep", split_axis=0, concat_axis=0, tiled=True
        ),
        lax.all_to_all(
            doubled(send_dy, expert_count, capacity), "ep", split_axis=0, concat_axis=0, tiled=True
        ),
        lax.all_to_all(
            doubled(send_gate, expert_count, capacity),
            "ep",
            split_axis=0,
            concat_axis=0,
            tiled=True,
        ),
    )
    rows_x = got_x.reshape(device_count, 2, capacity, feature_cols)
    rows_dy = got_dy.reshape(device_count, 2, capacity, feature_cols)
    rows_gate = got_gate.reshape(device_count, 2, capacity).astype(jnp.float32)
    up_pair = (w_up[0], copy_up[0])
    down_pair = (w_down[0], copy_down[0])
    row_tokens = tuple(
        (rows_x[:, member].reshape(device_count * capacity, feature_cols) for member in range(2))
    )
    row_cot = tuple(
        (rows_dy[:, member].reshape(device_count * capacity, feature_cols) for member in range(2))
    )
    row_gates = tuple(
        (rows_gate[:, member].reshape(device_count * capacity, 1) for member in range(2))
    )
    preact = lax.psum(
        tuple(
            (
                jnp.dot(row_tokens[member], up_pair[member], preferred_element_type=jnp.float32)
                for member in range(2)
            )
        ),
        "dp",
    )
    activations = tuple((jax.nn.silu(preact[member]).astype(jnp.bfloat16) for member in range(2)))
    upstream = lax.psum(
        tuple(
            (
                jnp.einsum(
                    "rd,hd->rh",
                    row_cot[member],
                    down_pair[member],
                    preferred_element_type=jnp.float32,
                )
                for member in range(2)
            )
        ),
        "dp",
    )
    dx_parts = []
    score_list = []
    up_grads = []
    down_grads = []
    for member in range(2):
        score_list.append(
            jnp.sum(activations[member].astype(jnp.float32) * upstream[member], axis=1).astype(
                jnp.bfloat16
            )
        )
        grad_preact = (row_gates[member] * upstream[member] * silu_slope(preact[member])).astype(
            jnp.bfloat16
        )
        scaled_cot = (row_gates[member] * row_cot[member].astype(jnp.float32)).astype(jnp.bfloat16)
        down_grads.append(
            jnp.einsum(
                "rh,rd->hd", activations[member], scaled_cot, preferred_element_type=jnp.float32
            )
        )
        up_grads.append(
            jnp.einsum(
                "rd,rh->dh", row_tokens[member], grad_preact, preferred_element_type=jnp.float32
            )
        )
        dx_parts.append(
            jnp.einsum(
                "rh,dh->rd", grad_preact, up_pair[member], preferred_element_type=jnp.float32
            ).astype(jnp.bfloat16)
        )
    back_up, back_down = passed_along(
        (up_grads[1].astype(jnp.bfloat16), down_grads[1].astype(jnp.bfloat16)),
        "ep",
        device_count // 2,
    )
    grad_up = (up_grads[0] + back_up.astype(jnp.float32)).astype(jnp.bfloat16)[None]
    grad_down = (down_grads[0] + back_down.astype(jnp.float32)).astype(jnp.bfloat16)[None]
    dx_buffer = jnp.stack(
        [piece.reshape(device_count, capacity, feature_cols) for piece in dx_parts], axis=1
    )
    score_buffer = jnp.stack(
        [piece.reshape(device_count, capacity) for piece in score_list], axis=1
    )
    back_rows, back_scores = (
        lax.all_to_all(dx_buffer, "ep", split_axis=0, concat_axis=0, tiled=True),
        lax.all_to_all(score_buffer, "ep", split_axis=0, concat_axis=0, tiled=True),
    )
    flat_rows = back_rows.reshape(-1, feature_cols)
    flat_scores = back_scores.reshape(-1)
    route_sum = jnp.zeros((tok_rows * route_count, feature_cols), jnp.float32)
    gate_total = jnp.zeros((tok_rows * route_count,), jnp.float32)
    for which_half in range(2):
        row_index = ((2 * target_pair + which_half) * 2 + copy_group) * capacity + slot_rank
        route_sum = route_sum + flat_rows[row_index].astype(jnp.float32)
        gate_total = gate_total + flat_scores[row_index].astype(jnp.float32)
    route_rows = lax.optimization_barrier(route_sum.astype(jnp.bfloat16)).astype(jnp.float32)
    grad_tokens = jnp.sum(route_rows.reshape(tok_rows, route_count, feature_cols), axis=1).astype(
        jnp.bfloat16
    )
    grad_gate = gate_total.reshape(tok_rows, route_count)
    return (grad_tokens, grad_gate, grad_up, grad_down)


def solution(mesh):
    in_specs = (
        P("ep", "dp"),
        P("ep", "dp"),
        P("ep", None),
        P("ep", None),
        P("ep", "dp", None),
        P("ep", None, "dp"),
    )
    out_specs = (P("ep", "dp"), P("ep", None), P("ep", "dp", None), P("ep", None, "dp"))
    return jax.shard_map(
        on_device, mesh=mesh, in_specs=in_specs, out_specs=out_specs, check_vma=False
    )
```

profile of v0, /device:TPU:2, one launch (start us, length us, event | category | flops | bytes accessed | tf_op | source)
XLA Modules:
  0.0 688.3 jit_solution(14291790630241767239)
XLA Ops:
  9.5 6.6 scatter_custom_fusion.2
  21.4 13.7 %all-to-all-start.2 = ((bf16[64,20,1792]{2,1,0:T(8,128)(2,1)}), bf16[64,20,1792]{2,1,0:T(8,128)(2,1)}, u32[]{:S(2)}, u32[]{:S(2)}) async-start(bf16[64,20,1792]{2,1,0:T(8,128)(2,1)} %bitcast.74), calls=%async_computation.2 | async-start | bytes 11010048 | tf_op jit(solution)/shard_map/all_to_all | solution.py:54
  35.1 6.9 %scatter_custom_fusion.1 = bf16[640,1792]{1,0:T(8,128)(2,1)} fusion(s32[256]{0:T(256)S(1)} %bitcast.84, bf16[]{:T(256)} %constant.50.clone.1, bf16[128,1792]{1,0:T(8,128)(2,1)} %param.7, s32[1024]{0:T(1024)S(1)} %pad_clamp_fusion.2), kind=kCustom, calls=%fused_computation.44 | custom fusion | bytes 2294272 | tf_op jit(solution)/shard_map/scatter | solution.py:50
  44.6 113.5 %all-to-all-done.2 = bf16[64,20,1792]{2,1,0:T(8,128)(2,1)} async-done(((bf16[64,20,1792]{2,1,0:T(8,128)(2,1)}), bf16[64,20,1792]{2,1,0:T(8,128)(2,1)}, u32[]{:S(2)}, u32[]{:S(2)}) %all-to-all-start.2) | async-done | bytes 4587552 | tf_op jit(solution)/shard_map/all_to_all | solution.py:54
  160.8 7.8 %all-to-all-start.1 = ((bf16[64,20,1792]{2,1,0:T(8,128)(2,1)}), bf16[64,20,1792]{2,1,0:T(8,128)(2,1)}, u32[]{:S(2)}, u32[]{:S(2)}) async-start(bf16[64,20,1792]{2,1,0:T(8,128)(2,1)} %bitcast.73), calls=%async_computation.1 | async-start | bytes 11010048 | tf_op jit(solution)/shard_map/all_to_all | solution.py:57
  179.3 5.7 reshape_squeeze.17
  185.0 106.5 %all-to-all-done.1 = bf16[64,20,1792]{2,1,0:T(8,128)(2,1)} async-done(((bf16[64,20,1792]{2,1,0:T(8,128)(2,1)}), bf16[64,20,1792]{2,1,0:T(8,128)(2,1)}, u32[]{:S(2)}, u32[]{:S(2)}) %all-to-all-start.1) | async-done | bytes 4587552 | tf_op jit(solution)/shard_map/all_to_all | solution.py:57
  299.9 5.3 reshape_squeeze.16
  308.3 5.5 reshape_squeeze.15
  320.8 4.6 fusion.11
  325.4 4.1 fusion.13
  329.5 4.1 fusion.6
  340.8 17.1 %all_to_all.29 = bf16[64,1,20]{2,1,0:T(2,128)(2,1)S(1)} all-to-all(bf16[64,1,20]{2,1,0:T(2,128)(2,1)S(1)} %copy.90), channel_id=1, replica_groups=mesh['ep'=64,'dp'=4] {'ep'}, dimensions={0} | all-to-all | bytes 5120 | tf_op jit(solution)/shard_map/all_to_all | solution.py:60
  358.5 91.9 %all-reduce.3.cloned.1.call-done = (f32[640,512]{1,0:T(8,128)}, f32[640,512]{1,0:T(8,128)}, f32[640,512]{1,0:T(8,128)}, f32[640,512]{1,0:T(8,128)}) async-done(((f32[640,512]{1,0:T(8,128)}, f32[640,512]{1,0:T(8,128)}, f32[640,512]{1,0:T(8,128)}, f32[640,512]{1,0:T(8,128)}), (f32[640,512]{1,0:T(8,128)}, f32[640,512]{1,0:T(8,128)}, f32[640,512]{1,0:T(8,128)}, ...) | async-done | bytes 5242896 | tf_op jit(solution)/shard_map/psum | solution.py:82
  450.5 4.5 multiply_reduce_fusion
  456.0 11.5 %all-to-all-start.4 = ((bf16[64,2,10]{2,1,0:T(2,128)(2,1)}), bf16[64,2,10]{2,1,0:T(2,128)(2,1)S(1)}, u32[]{:S(2)}, u32[]{:S(2)}) async-start(bf16[64,2,10]{2,1,0:T(2,128)(2,1)} %copy.102), calls=%async_computation.4 | async-start | bytes 65536 | tf_op jit(solution)/shard_map/all_to_all | solution.py:150
  467.4 4.3 convolution_convert_fusion.1
  471.8 5.3 stack_reshape.8
  477.0 4.5 convolution_convert_fusion
  481.5 5.2 stack_reshape.9
  486.7 7.1 %pad_maximum_fusion = bf16[64,2,10,1792]{3,2,0,1:T(8,128)(2,1)} fusion(bf16[64,1,10,1792]{3,2,0,1:T(8,128)(2,1)} %stack_reshape.9, bf16[64,1,10,1792]{3,2,0,1:T(8,128)(2,1)} %stack_reshape.8), kind=kLoop, calls=%fused_computation.9 | loop fusion | flops 2293760 | bytes 9175040 | tf_op jit(solution)/shard_map/stack | solution.py:142
  493.8 9.9 %copy.100 = bf16[64,2,10,1792]{3,1,2,0:T(2,128)(2,1)} copy(bf16[64,2,10,1792]{3,2,0,1:T(8,128)(2,1)} %pad_maximum_fusion) | data formatting | bytes 9175040 | tf_op jit(solution)/shard_map/stack | solution.py:142
  503.7 11.4 %all-to-all-start.3 = ((bf16[64,2,10,1792]{3,1,2,0:T(2,128)(2,1)}), bf16[64,2,10,1792]{3,1,2,0:T(2,128)(2,1)}, u32[]{:S(2)}, u32[]{:S(2)}) async-start(bf16[64,2,10,1792]{3,1,2,0:T(2,128)(2,1)} %copy.100), calls=%async_computation.3 | async-start | bytes 9175040 | tf_op jit(solution)/shard_map/all_to_all | solution.py:149
  515.1 4.8 convolution_convert_fusion.3
  531.4 70.2 %collective-permute-done.2 = bf16[1792,512]{1,0:T(8,128)(2,1)} collective-permute-done((bf16[1792,512]{1,0:T(8,128)(2,1)}, bf16[1792,512]{1,0:T(8,128)(2,1)}, u32[]{:S(2)}, u32[]{:S(2)}) %collective-permute-start.2) | collective-permute-done | bytes 1835040 | tf_op jit(solution)/shard_map/ppermute | solution.py:10
  601.6 5.0 fusion.4
  606.6 39.6 %collective-permute-done.3 = bf16[512,1792]{1,0:T(8,128)(2,1)} collective-permute-done((bf16[512,1792]{1,0:T(8,128)(2,1)}, bf16[512,1792]{1,0:T(8,128)(2,1)}, u32[]{:S(2)}, u32[]{:S(2)}) %collective-permute-start.3) | collective-permute-done | bytes 1835040 | tf_op jit(solution)/shard_map/ppermute | solution.py:10
  646.2 4.5 fusion.1
  650.7 6.8 copy.101
  657.5 9.6 %reshape.293 = bf16[1280,1792]{1,0:T(8,128)(2,1)} reshape(bf16[64,2,10,1792]{3,2,1,0:T(8,128)(2,1)} %copy.101) | data formatting | bytes 9175040 | tf_op jit(solution)/shard_map/reshape | solution.py:152
  667.1 5.0 gather_fusion
  672.1 5.0 gather_fusion.1
  (86 shorter events, 65.9 us)
Async XLA Ops:
  7.2 2.3 copy-start
  21.4 136.7 %all-to-all-start.2 = ((bf16[64,20,1792]{2,1,0:T(8,128)(2,1)}), bf16[64,20,1792]{2,1,0:T(8,128)(2,1)}, u32[]{:S(2)}, u32[]{:S(2)}) async-start(bf16[64,20,1792]{2,1,0:T(8,128)(2,1)} %bitcast.74), calls=%async_computation.2 | async-start | bytes 11010048 | tf_op jit(solution)/shard_map/all_to_all | solution.py:54
  160.8 130.7 %all-to-all-start.1 = ((bf16[64,20,1792]{2,1,0:T(8,128)(2,1)}), bf16[64,20,1792]{2,1,0:T(8,128)(2,1)}, u32[]{:S(2)}, u32[]{:S(2)}) async-start(bf16[64,20,1792]{2,1,0:T(8,128)(2,1)} %bitcast.73), calls=%async_computation.1 | async-start | bytes 11010048 | tf_op jit(solution)/shard_map/all_to_all | solution.py:57
  168.6 281.8 %all-reduce.3.cloned.1.call-start = ((), (), s32[]{:S(2)}) async-start(), calls=%async_computation.5 | async-start | bytes 10485760 | tf_op jit(solution)/shard_map/psum | solution.py:82
  168.7 160.8 %collective-permute-start.1 = (bf16[1,1792,512]{2,1,0:T(8,128)(2,1)}, bf16[1,1792,512]{2,1,0:T(8,128)(2,1)}, u32[]{:S(2)}, u32[]{:S(2)}) collective-permute-start(bf16[1,1792,512]{2,1,0:T(8,128)(2,1)} %param.10), channel_id=1, source_target_pairs={{0,128},{4,132},{8,136},{12,140},{16,144},{20,148},{24,152},{28,15... | collective-permute-start | bytes 5505032 | tf_op jit(solution)/shard_map/ppermute | solution.py:10
  171.9 161.7 %collective-permute-start = (bf16[1,512,1792]{2,1,0:T(8,128)(2,1)}, bf16[1,512,1792]{2,1,0:T(8,128)(2,1)}, u32[]{:S(2)}, u32[]{:S(2)}) collective-permute-start(bf16[1,512,1792]{2,1,0:T(8,128)(2,1)} %param.11), channel_id=1, source_target_pairs={{0,128},{4,132},{8,136},{12,140},{16,144},{20,148},{24,152},{28,15... | collective-permute-start | bytes 5505032 | tf_op jit(solution)/shard_map/ppermute | solution.py:10
  308.3 5.5 copy-start.2
  325.4 4.1 copy-start.3
  329.5 4.1 copy-start.4
  337.5 0.7 copy-start.8
  456.0 47.7 %all-to-all-start.4 = ((bf16[64,2,10]{2,1,0:T(2,128)(2,1)}), bf16[64,2,10]{2,1,0:T(2,128)(2,1)S(1)}, u32[]{:S(2)}, u32[]{:S(2)}) async-start(bf16[64,2,10]{2,1,0:T(2,128)(2,1)} %copy.102), calls=%async_computation.4 | async-start | bytes 65536 | tf_op jit(solution)/shard_map/all_to_all | solution.py:150
  503.7 147.0 %all-to-all-start.3 = ((bf16[64,2,10,1792]{3,1,2,0:T(2,128)(2,1)}), bf16[64,2,10,1792]{3,1,2,0:T(2,128)(2,1)}, u32[]{:S(2)}, u32[]{:S(2)}) async-start(bf16[64,2,10,1792]{3,1,2,0:T(2,128)(2,1)} %copy.100), calls=%async_computation.3 | async-start | bytes 9175040 | tf_op jit(solution)/shard_map/all_to_all | solution.py:149
  515.1 7.9 %copy-start.5 = (bf16[640,1792]{1,0:T(8,128)(2,1)S(1)}, bf16[640,1792]{1,0:T(8,128)(2,1)}, u32[]{:S(2)}) copy-start(bf16[640,1792]{1,0:T(8,128)(2,1)} %reshape_squeeze.16) | copy-start | bytes 6881284
  515.1 7.9 %copy-start.7 = (f32[640,512]{1,0:T(8,128)S(1)}, f32[640,512]{1,0:T(8,128)}, u32[]{:S(2)}) copy-start(f32[640,512]{1,0:T(8,128)} %get-tuple-element.24) | copy-start | bytes 3932164
  519.9 81.7 %collective-permute-start.2 = (bf16[1792,512]{1,0:T(8,128)(2,1)}, bf16[1792,512]{1,0:T(8,128)(2,1)}, u32[]{:S(2)}, u32[]{:S(2)}) collective-permute-start(bf16[1792,512]{1,0:T(8,128)(2,1)} %convolution_convert_fusion.3), channel_id=1, source_target_pairs={{0,128},{4,132},{8,136},{12,140},{16,144},{20,148},{24,152},{28,15... | collective-permute-start | bytes 5505032 | tf_op jit(solution)/shard_map/ppermute | solution.py:10
  526.1 120.1 %collective-permute-start.3 = (bf16[512,1792]{1,0:T(8,128)(2,1)}, bf16[512,1792]{1,0:T(8,128)(2,1)}, u32[]{:S(2)}, u32[]{:S(2)}) collective-permute-start(bf16[512,1792]{1,0:T(8,128)(2,1)} %convolution_convert_fusion.2), channel_id=1, source_target_pairs={{0,128},{4,132},{8,136},{12,140},{16,144},{20,148},{24,152},{28,15... | collective-permute-start | bytes 5505032 | tf_op jit(solution)/shard_map/ppermute | solution.py:10
  531.4 114.8 %copy-start.6 = (f32[640,512]{1,0:T(8,128)S(1)}, f32[640,512]{1,0:T(8,128)}, u32[]{:S(2)}) copy-start(f32[640,512]{1,0:T(8,128)} %get-tuple-element.26) | copy-start | bytes 3932164
  677.2 3.8 copy-start.1
Sparse Core Ops, SparseCore 0:
  337.7 112.7 all-reduce.2
where the time goes:
time: 696 us; the launch traced here: 688 us
  waiting for transfers between devices  422 us (61%)
  local copies, waits for them, and re-layouts  124 us (18%)
  starting transfers between devices  51.6 us (7%)
  matrix products  42.9 us (6%)
  blocking collectives  17.1 us (2%)
  other arithmetic  15.9 us (2%)
  between operations  14.8 us (2%)
    all_to_all x1, waiting for transfers between devices, on_device(): lax.all_to_all(doubled(send_x, expert_count, capacity), 'ep', split_axis=...  113 us
    ppermute x4, waiting for transfers between devices, passed_along(): return lax.ppermute(value, axis, pairs)  110 us
    all_to_all x1, waiting for transfers between devices, on_device(): lax.all_to_all(doubled(send_dy, expert_count, capacity), 'ep', split_axis...  107 us
    psum x1, waiting for transfers between devices, on_device(): lax.psum(tuple((jnp.dot(row_tokens[member], up_pair[member], preferred_el...  91.9 us
    another operation x3, local copies, waits for them, and re-layouts, on_device(): jnp.stack([piece.reshape(device_count, capacity, feature_cols) for piece...  20.3 us
    all_to_all x1, blocking collectives, on_device(): lax.all_to_all(doubled(send_gate, expert_count, capacity), 'ep', split_ax...  17.1 us
  transfers between devices with their start and end apart: 9, of which 5 were waited for; matrix products, arithmetic and copies ran while one was open for 18% of the time, Pallas kernels for 0%

commit v1 on v0

v1 whole, which is shorter than its diff:
```python
import functools

import jax
import jax.numpy as jnp
from jax import lax
from jax.experimental import pallas as pl
from jax.experimental.pallas import tpu as pltpu
from jax.sharding import PartitionSpec as P

MESH = pl.DeviceIdType.MESH
F32, BF16 = jnp.float32, jnp.bfloat16
NY, NX, NZ = 4, 2, 8
NO = NY * NX
CAP = 10
TR = 16
TILES = NZ * CAP // TR
BR = NO * TR
DISP = (0, -1, 1, -2, 2, -3, 3, 4)
SPANS = tuple(
    tuple(sorted({(TR * t + i) // CAP for i in range(TR)})) for t in range(TILES)
)
FAR_TO_NEAR = ((7, 6, 4, 2), (7, 5, 3, 1))
LC = 256


def dot(a, b, ca=1, cb=0):
    return lax.dot_general(a, b, (((ca,), (cb,)), ((), ())), preferred_element_type=F32)


def kernel(
    x_ref, c_ref, info_ref, up_ref, down_ref,
    gx_ref, gs_ref, gu_ref, gd_ref,
    xa, ca, ma, smat, gmat, sx, rx, puf, own, ps, pr, qs, qr, ag, dxs, dxr,
    r0o, r0i, rso, rsi, sco, sci, tf,
    ag_s, ag_r, yx_s, yx_r, dp_s, dp_r, rt_s, rt_r, rs_s, rs_r, sc_s, sc_r,
):
    tok, dl = x_ref.shape
    hid = up_ref.shape[1]
    half_rows = BR // 2
    half_lanes = dl // 2
    me = lax.axis_index("ep")
    dp = lax.axis_index("dp")
    z, yx = me % NZ, me // NZ
    y, x = yx // NX, yx % NX
    core, hi = dp % 2, dp // 2
    neighbour = (yx * NZ + (z + 1) % NZ, yx * NZ + (z + NZ - 1) % NZ)
    core_peer, hi_peer = hi * 2 + (1 - core), (1 - hi) * 2 + core

    def at_offset(o, sign):
        dy, dx = o // NX, o % NX
        there = ((y + sign * dy + NY) % NY) * NX + (x + sign * dx + NX) % NX
        return there * NZ + z

    def remote(src, dst, ss, rs, device):
        return pltpu.make_async_remote_copy(
            src_ref=src, dst_ref=dst, send_sem=ss, recv_sem=rs, device_id=device, device_id_type=MESH
        )

    barrier = pltpu.get_barrier_semaphore()
    peers = [{"ep": n} for n in neighbour]
    peers += [{"ep": at_offset(o, 1)} for o in range(1, NO)]
    peers += [{"dp": core_peer}, {"dp": hi_peer}]
    for peer in peers:
        pl.semaphore_signal(barrier, inc=1, device_id=peer, device_id_type=MESH)

    info = info_ref[...]
    ids = [info[k : k + 1, :] for k in range(2)]
    expert_no = lax.broadcasted_iota(jnp.int32, (NO * NZ // 2, tok), 0).astype(F32)
    hot = [jnp.where(expert_no == ids[k], 1.0, 0.0) for k in range(2)]
    earlier = lax.broadcasted_iota(jnp.int32, (tok, tok), 0) < lax.broadcasted_iota(
        jnp.int32, (tok, tok), 1
    )
    before = dot((hot[0] + hot[1]).astype(BF16), jnp.where(earlier, 1.0, 0.0).astype(BF16))
    code = [
        ids[k] * 16.0 + jnp.sum(before * hot[k], axis=0, keepdims=True) for k in range(2)
    ]
    line = lax.broadcasted_iota(jnp.int32, (8, tok), 0)
    ma[0:8, :] = jnp.where(line == 0, code[0], jnp.where(line == 1, code[1], info))
    pl.semaphore_wait(barrier, len(peers))

    def block(ref, own_ref, j):
        return own_ref if j == 0 else ref.at[(j - 1) * tok : j * tok, :]

    def gather_sent(way, step, n):
        return step < 3 or n == way or (way == 0 and n == 2)

    def gather_copy(way, step, n):
        src = 0 if step == 0 else 2 * step - 1 + way
        dst = 7 if step == 3 else 2 * step + 1 + way
        if n == 2:
            a, b = ma.at[src * 8 : src * 8 + 8, :], ma.at[dst * 8 : dst * 8 + 8, :]
        else:
            ref, own_ref = ((xa, x_ref), (ca, c_ref))[n]
            a, b = block(ref, own_ref, src), block(ref, own_ref, dst)
        sem = (way * 4 + step) * 3 + n
        return remote(a, b, ag_s.at[sem], ag_r.at[sem], {"ep": neighbour[way]})

    def gather_start(step):
        for n in range(3):
            for way in range(2):
                gather_copy(way, step, n).start()

    def gather_next(step):
        for n in range(3):
            for way in range(2):
                if gather_sent(way, step, n):
                    gather_copy(way, step, n).wait_recv()
                if step < 3 and gather_sent(way, step + 1, n):
                    gather_copy(way, step + 1, n).start()

    rho = lax.broadcasted_iota(jnp.int32, (BR, tok), 0)
    o_of = rho >> 4
    i_of = rho & 15
    to_yx = ((y + (o_of >> 1)) & (NY - 1)) * NX + ((x + (o_of & 1)) & (NX - 1))
    expert_of = to_yx * (NZ // 2) + z // 2

    def matches(t, j):
        rank = i_of + (TR * t - CAP * j)
        good = jnp.logical_and(rank >= 0, rank < CAP)
        want = jnp.where(good, expert_of * 16 + rank, -1).astype(F32)
        return [want == ma[j * 8 + k : j * 8 + k + 1, :] for k in range(2)]

    def rows_of(t):
        return pl.ds(t * BR, BR)

    def yx_copy(t, o):
        rows = pl.ds(t * BR + o * TR, TR)
        return remote(sx.at[rows, :], rx.at[rows, :], yx_s.at[t], yx_r.at[t], {"ep": at_offset(o, 1)})

    def yx_all(t):
        rows = pl.ds(t * BR + TR, BR - TR)
        return remote(sx.at[rows, :], rx.at[rows, :], yx_s.at[t], yx_r.at[t], {"ep": at_offset(1, 1)})

    def select(t):
        for n, j in enumerate(SPANS[t]):
            first, second = matches(t, j)
            lanes = pl.ds(n * tok, tok)
            smat[rows_of(t), lanes] = jnp.where(jnp.logical_or(first, second), 1.0, 0.0).astype(BF16)
            gates = [ma[j * 8 + 2 + k : j * 8 + 3 + k, :] for k in range(2)]
            gmat[:, lanes] = jnp.where(first, gates[0], jnp.where(second, gates[1], 0.0)).astype(BF16)

        def part(i, carry):
            lanes = pl.ds(pl.multiple_of(i * LC, LC), LC)
            later = pl.ds(pl.multiple_of(dl + i * LC, LC), LC)
            for pick, ref, own_ref, out in ((smat, xa, x_ref, lanes), (gmat, ca, c_ref, later)):
                total = None
                for n, j in enumerate(SPANS[t]):
                    chosen = pick[rows_of(t) if pick is smat else slice(0, BR), n * tok : (n + 1) * tok]
                    one = dot(chosen, block(ref, own_ref, j)[:, lanes])
                    total = one if total is None else total + one
                sx[rows_of(t), out] = total.astype(BF16)
            return carry

        lax.fori_loop(0, dl // LC, part, 0)
        for o in range(1, NO):
            yx_copy(t, o).start()
        rx[t * BR : t * BR + TR, :] = sx[t * BR : t * BR + TR, :]

    def dp_copy(t, stage):
        sems = (dp_s.at[t * 3 + stage], dp_r.at[t * 3 + stage])
        here = pl.ds(t * half_rows, half_rows)
        if stage == 0:
            return remote(ps.at[here, :], pr.at[here, :], *sems, {"dp": core_peer})
        if stage == 1:
            return remote(qs.at[here, :], qr.at[here, :], *sems, {"dp": hi_peer})
        mine = pl.ds(pl.multiple_of(t * BR + core * half_rows, half_rows), half_rows)
        return remote(ag.at[mine, :], ag.at[mine, :], *sems, {"dp": core_peer})

    def hidden(t):
        yx_all(t).wait_recv()

        def part(i, carry):
            cols = pl.ds(pl.multiple_of(i * LC, LC), LC)
            later = pl.ds(pl.multiple_of(hid + i * LC, LC), LC)
            puf[:, cols] = dot(rx[rows_of(t), 0:dl], up_ref[:, cols])
            puf[:, later] = dot(rx[rows_of(t), dl : 2 * dl], down_ref[cols, :], 1, 1)
            return carry

        lax.fori_loop(0, hid // LC, part, 0)
        here = pl.ds(t * half_rows, half_rows)
        theirs = pl.ds(pl.multiple_of((1 - core) * half_rows, half_rows), half_rows)
        mine = pl.ds(pl.multiple_of(core * half_rows, half_rows), half_rows)
        ps[here, :] = puf[theirs, :].astype(BF16)
        dp_copy(t, 0).start()
        own[here, :] = puf[mine, :]

    def chip_sum(t):
        dp_copy(t, 0).wait_recv()
        here = pl.ds(t * half_rows, half_rows)
        qs[here, :] = (own[here, :] + pr[here, :].astype(F32)).astype(BF16)
        dp_copy(t, 1).start()

    def activate(t):
        dp_copy(t, 1).wait_recv()
        here = pl.ds(t * half_rows, half_rows)
        mine = pl.ds(pl.multiple_of(t * BR + core * half_rows, half_rows), half_rows)
        preact = qs[here, 0:hid].astype(F32) + qr[here, 0:hid].astype(F32)
        upstream = qs[here, hid : 2 * hid].astype(F32) + qr[here, hid : 2 * hid].astype(F32)
        sig = 1.0 / (1.0 + jnp.exp(-preact))
        act = (preact * sig).astype(BF16)
        ag[mine, 0:hid] = act
        ag[mine, hid : 2 * hid] = (upstream * (sig * (1.0 + preact * (1.0 - sig)))).astype(BF16)
        score = jnp.sum(act.astype(F32) * upstream, axis=1, keepdims=True)
        ag[mine, 2 * hid : 2 * hid + 128] = jnp.broadcast_to(score, (half_rows, 128)).astype(BF16)
        dp_copy(t, 2).start()

    def back_copy(t, o):
        rows = pl.ds(t * BR + o * TR, TR)
        return remote(dxs.at[rows, :], dxr.at[rows, :], rt_s.at[t], rt_r.at[t], {"ep": at_offset(o, -1)})

    def back_all(t):
        rows = pl.ds(t * BR + TR, BR - TR)
        return remote(dxs.at[rows, :], dxr.at[rows, :], rt_s.at[t], rt_r.at[t], {"ep": at_offset(1, -1)})

    def send_back(t):
        dp_copy(t, 2).wait_recv()

        def part(i, carry):
            cols = pl.ds(pl.multiple_of(i * LC, LC), LC)
            dxs[rows_of(t), cols] = dot(ag[rows_of(t), hid : 2 * hid], up_ref[cols, :], 1, 1).astype(BF16)
            return carry

        lax.fori_loop(0, dl // LC, part, 0)
        dxs[rows_of(t), dl : dl + 128] = ag[rows_of(t), 2 * hid : 2 * hid + 128]
        for o in range(1, NO):
            back_copy(t, o).start()
        dxr[t * BR : t * BR + TR, :] = dxs[t * BR : t * BR + TR, :]

    def token_sum(j, lo, hi_lane):
        total = None
        for t in range(TILES):
            if j in SPANS[t]:
                n = SPANS[t].index(j)
                one = dot(smat[rows_of(t), n * tok : (n + 1) * tok], dxr[rows_of(t), lo:hi_lane], 0, 0)
                total = one if total is None else total + one
        return total

    def score_sum(j):
        sums = [0.0, 0.0]
        for t in range(TILES):
            if j in SPANS[t]:
                value = dxr[rows_of(t), dl : dl + 128].astype(F32)
                for k, hit in enumerate(matches(t, j)):
                    sums[k] = sums[k] + jnp.sum(jnp.where(hit, value, 0.0), axis=0, keepdims=True)
        return jnp.where(line == 0, sums[0], jnp.where(line == 1, sums[1], 0.0))

    def sum_copy(way, step):
        n = way * 4 + step
        sems = (rs_s.at[n], rs_r.at[n])
        if step == 0:
            rows = pl.ds(way * tok, tok)
            return remote(r0o.at[rows, :], r0i.at[rows, :], *sems, {"ep": neighbour[way]})
        rows = pl.ds((way * 3 + step - 1) * tok, tok)
        return remote(rso.at[rows, :], rsi.at[rows, :], *sems, {"ep": neighbour[way]})

    def score_copy(way, step):
        n = way * 4 + step
        rows = pl.ds(n * 8, 8)
        return remote(sco.at[rows, :], sci.at[rows, :], sc_s.at[n], sc_r.at[n], {"ep": neighbour[way]})

    def scored(way, step):
        return step > 0 or way == 0

    def sum_first():
        for way in range(2):
            lo = way * half_lanes
            r0o[way * tok : (way + 1) * tok, :] = token_sum(7, lo, lo + half_lanes).astype(BF16)
            sum_copy(way, 0).start()
        sco[0:8, :] = score_sum(7)
        score_copy(0, 0).start()

    def sum_ready(way, step):
        j = FAR_TO_NEAR[way][step]
        for lo in (0, half_lanes):
            tf[way * tok : (way + 1) * tok, lo : lo + half_lanes] = token_sum(j, lo, lo + half_lanes)
        n = way * 4 + step
        sco[n * 8 : n * 8 + 8, :] = score_sum(j)

    def sum_next(way, step):
        mine = slice(way * tok, (way + 1) * tok)
        out = slice((way * 3 + step - 1) * tok, (way * 3 + step) * tok)
        sum_copy(way, step - 1).wait_recv()
        if step == 1:
            lo = way * half_lanes
            other = half_lanes - lo
            rso[out, lo : lo + half_lanes] = (
                tf[mine, lo : lo + half_lanes] + r0i[mine, :].astype(F32)
            ).astype(BF16)
            rso[out, other : other + half_lanes] = tf[mine, other : other + half_lanes].astype(BF16)
        else:
            came = slice((way * 3 + step - 2) * tok, (way * 3 + step - 1) * tok)
            rso[out, :] = (tf[mine, :] + rsi[came, :].astype(F32)).astype(BF16)
        sum_copy(way, step).start()
        n = way * 4 + step
        if scored(way, step - 1):
            score_copy(way, step - 1).wait_recv()
            sco[n * 8 : n * 8 + 8, :] += sci[n * 8 - 8 : n * 8, :]
        score_copy(way, step).start()

    def up_gradient():
        def part(i, carry):
            cols = pl.ds(pl.multiple_of(i * LC, LC), LC)
            gu_ref[cols, :] = dot(rx[:, cols], ag[:, hid : 2 * hid], 0, 0).astype(BF16)
            return carry

        lax.fori_loop(0, dl // LC, part, 0)

    def down_gradient():
        def part(i, carry):
            cols = pl.ds(pl.multiple_of(i * LC, LC), LC)
            later = pl.ds(pl.multiple_of(dl + i * LC, LC), LC)
            gd_ref[:, cols] = dot(ag[:, 0:hid], rx[:, later], 0, 0).astype(BF16)
            return carry

        lax.fori_loop(0, dl // LC, part, 0)

    gather_start(0)
    gather_next(0)
    select(0)
    gather_next(1)
    select(1)
    select(2)
    hidden(0)
    chip_sum(0)
    activate(0)
    send_back(0)
    gather_next(2)
    select(3)
    hidden(1)
    hidden(2)
    chip_sum(1)
    chip_sum(2)
    gather_next(3)
    select(4)
    activate(1)
    activate(2)
    hidden(3)
    send_back(1)
    chip_sum(3)
    send_back(2)
    activate(3)
    hidden(4)
    chip_sum(4)
    send_back(3)
    activate(4)
    send_back(4)
    for t in range(TILES):
        back_all(t).wait_recv()
    sum_first()
    for step in range(1, 4):
        for way in range(2):
            sum_ready(way, step)
        for way in range(2):
            sum_next(way, step)
        if step == 1:
            up_gradient()
        if step == 2:
            down_gradient()
    for lo in (0, half_lanes):
        tf[0:tok, lo : lo + half_lanes] = token_sum(0, lo, lo + half_lanes)
    scores = score_sum(0)
    for way in range(2):
        sum_copy(way, 3).wait_recv()
        score_copy(way, 3).wait_recv()
    gx_ref[...] = (
        tf[0:tok, :] + rsi[2 * tok : 3 * tok, :].astype(F32) + rsi[5 * tok : 6 * tok, :].astype(F32)
    ).astype(BF16)
    gates = jnp.where(line == 0, ma[2:3, :], jnp.where(line == 1, ma[3:4, :], 1.0))
    gs_ref[...] = (scores + sci[24:32, :] + sci[56:64, :]) / gates

    for way in range(2):
        for step in range(4):
            for n in range(3):
                if gather_sent(way, step, n):
                    gather_copy(way, step, n).wait_send()
            sum_copy(way, step).wait_send()
            if scored(way, step):
                score_copy(way, step).wait_send()
    for t in range(TILES):
        yx_all(t).wait_send()
        back_all(t).wait_send()
        for stage in range(3):
            dp_copy(t, stage).wait_send()


def on_device(tokens, cotangent, gate_prob, expert_ids, w_up, w_down):
    tok, dl = tokens.shape
    hid = w_up.shape[2]
    info = jnp.concatenate(
        [expert_ids.astype(F32), gate_prob.astype(F32), jnp.zeros((tok, 4), F32)], axis=1
    ).T
    vmem = pl.BlockSpec(memory_space=pltpu.VMEM)
    rows = TILES * BR
    halves = rows // 2
    wide = max(len(s) for s in SPANS) * tok
    scratch = [
        pltpu.VMEM((7 * tok, dl), BF16),
        pltpu.VMEM((7 * tok, dl), BF16),
        pltpu.VMEM((8 * 8, tok), F32),
        pltpu.VMEM((rows, wide), BF16),
        pltpu.VMEM((BR, wide), BF16),
        pltpu.VMEM((rows, 2 * dl), BF16),
        pltpu.VMEM((rows, 2 * dl), BF16),
        pltpu.VMEM((BR, 2 * hid), F32),
        pltpu.VMEM((halves, 2 * hid), F32),
        pltpu.VMEM((halves, 2 * hid), BF16),
        pltpu.VMEM((halves, 2 * hid), BF16),
        pltpu.VMEM((halves, 2 * hid), BF16),
        pltpu.VMEM((halves, 2 * hid), BF16),
        pltpu.VMEM((rows, 2 * hid + 128), BF16),
        pltpu.VMEM((rows, dl + 128), BF16),
        pltpu.VMEM((rows, dl + 128), BF16),
        pltpu.VMEM((2 * tok, dl // 2), BF16),
        pltpu.VMEM((2 * tok, dl // 2), BF16),
        pltpu.VMEM((6 * tok, dl), BF16),
        pltpu.VMEM((6 * tok, dl), BF16),
        pltpu.VMEM((8 * 8, tok), F32),
        pltpu.VMEM((8 * 8, tok), F32),
        pltpu.VMEM((2 * tok, dl), F32),
    ]
    for count in (24, TILES, 3 * TILES, TILES, 8, 8):
        scratch += [pltpu.SemaphoreType.DMA((count,))] * 2
    grad_tokens, scores, grad_up, grad_down = pl.pallas_call(
        kernel,
        out_shape=(
            jax.ShapeDtypeStruct((tok, dl), BF16),
            jax.ShapeDtypeStruct((8, tok), F32),
            jax.ShapeDtypeStruct((dl, hid), BF16),
            jax.ShapeDtypeStruct((hid, dl), BF16),
        ),
        in_specs=[vmem] * 5,
        out_specs=(vmem,) * 4,
        scratch_shapes=scratch,
        compiler_params=pltpu.CompilerParams(
            collective_id=0, has_side_effects=True, vmem_limit_bytes=60 * 2**20
        ),
    )(tokens, cotangent, info, w_up[0], w_down[0])
    return grad_tokens, scores[:2].T, grad_up[None], grad_down[None]


def solution(mesh):
    in_specs = (
        P("ep", "dp"),
        P("ep", "dp"),
        P("ep", None),
        P("ep", None),
        P("ep", "dp", None),
        P("ep", None, "dp"),
    )
    out_specs = (P("ep", "dp"), P("ep", None), P("ep", "dp", None), P("ep", None, "dp"))
    return jax.shard_map(
        on_device, mesh=mesh, in_specs=in_specs, out_specs=out_specs, check_vma=False
    )
```

time: 696 us -> 197 us (0.28); the launches traced: 688 us -> 197 us
  waiting for transfers between devices: 422 us -> 0 us
  Pallas kernels: 0 us -> 187 us
  local copies, waits for them, and re-layouts: 124 us -> 7.34 us
  starting transfers between devices: 51.6 us -> 0 us
  matrix products: 42.9 us -> 0 us
  blocking collectives: 17.1 us -> 0 us
  between operations: 14.8 us -> 0.65 us
  other arithmetic: 15.9 us -> 2 us
    all_to_all x4 -> x0, waiting for transfers between devices: 220 us -> none  [the longest x1 113 us: on_device(): lax.all_to_all(doubled(send_x, expert_count, capacity), 'ep', split_axis=...]
    pallas_call x0 -> x1, Pallas kernels: none -> 187 us  [on_device(): pl.pallas_call(kernel, out_shape=(jax.ShapeDtypeStruct((tok, dl), BF16),...]
    ppermute x4 -> x0, waiting for transfers between devices: 110 us -> none  [passed_along(): return lax.ppermute(value, axis, pairs)]
    psum x1 -> x0, waiting for transfers between devices: 91.9 us -> none  [on_device(): lax.psum(tuple((jnp.dot(row_tokens[member], up_pair[member], preferred_el...]
    all_to_all x4 -> x0, starting transfers between devices: 44.4 us -> none  [the longest x1 13.7 us: on_device(): lax.all_to_all(doubled(send_x, expert_count, capacity), 'ep', split_axis=...]
    dot_general x10 -> x0, matrix products: 42.9 us -> none  [the longest x2 9.83 us: on_device(): jnp.einsum('rd,rh->dh', row_tokens[member], grad_preact, preferred_elemen...]
    another operation x9 -> x0, local copies, waits for them, and re-layouts: 41.3 us -> none  [the longest x3 20.3 us: on_device(): jnp.stack([piece.reshape(device_count, capacity, feature_cols) for piece...]
    all_to_all x1 -> x0, blocking collectives: 17.1 us -> none  [on_device(): lax.all_to_all(doubled(send_gate, expert_count, capacity), 'ep', split_ax...]
  transfers between devices with their start and end apart: 9 -> 0, of which waited for: 5 -> 0; matrix products, arithmetic and copies ran while one was open for 18% -> 0% of each run, Pallas kernels for 0% -> 0%
where the time goes in v1:
time: 197 us
  Pallas kernels  187 us (95%)
  local copies, waits for them, and re-layouts  7.34 us (4%)
  other arithmetic  2 us (1%)
    pallas_call x1, Pallas kernels, on_device(): pl.pallas_call(kernel, out_shape=(jax.ShapeDtypeStruct((tok, dl), BF16),...  187 us
    unnamed x5, local copies, waits for them, and re-layouts  6.03 us

profile of v1, /device:TPU:2, one launch (start us, length us, event | category | flops | bytes accessed | tf_op | source)
XLA Modules:
  0.0 197.0 jit_solution(2964462218775618309)
XLA Ops:
  0.6 0.1 pad.2.clone
  0.7 0.7 convert_element_type.7
  1.4 0.7 convert_element_type.6
  2.1 0.7 maximum_bitcast_fusion.info_ref
  2.7 187.0 %shard_map.93 = (bf16[128,1792]{1,0:T(8,128)(2,1)}, f32[8,128]{1,0:T(8,128)}, bf16[1792,512]{1,0:T(8,128)(2,1)}, bf16[512,1792]{1,0:T(8,128)(2,1)}) custom-call(bf16[128,1792]{1,0:T(8,128)(2,1)} %x_ref.1, bf16[128,1792]{1,0:T(8,128)(2,1)} %c_ref.1, f32[8,128]{1,0:T(8,128)} %maximum_bitcast_fusion.info_ref, bf16[1792,512]{1,0:T(8,128)(2,1)} %bitcast.10, ...), custom_call_target="tpu_custom_call" | custom-call | tf_op jit(solution)/shard_map/pallas_call | solution.py:423
  189.7 1.2 slice_bitcast_fusion
  190.9 1.8 copy.13
  192.8 0.0 copy-start
  192.8 3.0 %copy.14 = bf16[1,1792,512]{2,1,0:T(8,128)(2,1)} copy(bf16[1,1792,512]{2,1,0:T(8,128)(2,1)} %bitcast.9) | data formatting | bytes 3670016
  195.7 0.0 copy-done
  195.7 1.2 copy.15
  (1 shorter events, 0.0 us)
Async XLA Ops:
  192.8 3.0 %copy-start = (bf16[512,1792]{1,0:T(8,128)(2,1)S(1)}, bf16[512,1792]{1,0:T(8,128)(2,1)}, u32[]{:S(2)}) copy-start(bf16[512,1792]{1,0:T(8,128)(2,1)} %get-tuple-element.11) | copy-start | bytes 5505028

commit v2 on v1

v2 whole, which is shorter than its diff:
```python
import functools

import jax
import jax.numpy as jnp
from jax import lax
from jax.experimental import pallas as pl
from jax.experimental.pallas import tpu as pltpu
from jax.sharding import PartitionSpec as P

MESH = pl.DeviceIdType.MESH
F32, BF16 = jnp.float32, jnp.bfloat16
NY, NX, NZ = 4, 2, 8
NO = NY * NX
CAP = 10
TR = 16
TILES = NZ * CAP // TR
BR = NO * TR
DISP = (0, -1, 1, -2, 2, -3, 3, 4)
SPANS = tuple(
    tuple(sorted({(TR * t + i) // CAP for i in range(TR)})) for t in range(TILES)
)
FAR_TO_NEAR = ((7, 6, 4, 2), (7, 5, 3, 1))
LC = 256


def dot(a, b, ca=1, cb=0):
    return lax.dot_general(a, b, (((ca,), (cb,)), ((), ())), preferred_element_type=F32)


def kernel(
    x_ref, c_ref, gate_ref, ids_ref, up_hbm, down_hbm,
    gx_ref, gs_ref, gu_hbm, gd_hbm,
    xa, ca, ma, smat, gmat, sx, rx, puf, own, ps, pr, qs, qr, ag, dxs, dxr,
    rso, rsi, sco, sci, tf, up_ref, down_ref, gu_ref, gd_ref, w_s,
    ag_s, ag_r, yx_s, yx_r, dp_s, dp_r, rt_s, rt_r, rs_s, rs_r, sc_s, sc_r,
):
    tok, dl = x_ref.shape
    hid = up_ref.shape[1]
    slots = TILES * BR
    half_rows = BR // 2
    half_lanes = dl // 2
    me = lax.axis_index("ep")
    dp = lax.axis_index("dp")
    z, yx = me % NZ, me // NZ
    y, x = yx // NX, yx % NX
    core, hi = dp % 2, dp // 2
    neighbour = (yx * NZ + (z + 1) % NZ, yx * NZ + (z + NZ - 1) % NZ)
    core_peer, hi_peer = hi * 2 + (1 - core), (1 - hi) * 2 + core

    def at_offset(o, sign):
        dy, dx = o // NX, o % NX
        there = ((y + sign * dy + NY) % NY) * NX + (x + sign * dx + NX) % NX
        return there * NZ + z

    def remote(src, dst, ss, rs, device):
        return pltpu.make_async_remote_copy(
            src_ref=src, dst_ref=dst, send_sem=ss, recv_sem=rs, device_id=device, device_id_type=MESH
        )

    barrier = pltpu.get_barrier_semaphore()
    peers = [{"ep": n} for n in neighbour]
    peers += [{"ep": at_offset(o, 1)} for o in range(1, NO)]
    peers += [{"dp": core_peer}, {"dp": hi_peer}]
    for peer in peers:
        pl.semaphore_signal(barrier, inc=1, device_id=peer, device_id_type=MESH)

    loads = [
        pltpu.make_async_copy(up_hbm, up_ref, w_s.at[0]),
        pltpu.make_async_copy(down_hbm, down_ref, w_s.at[1]),
    ]
    for load in loads:
        load.start()

    eye = jnp.where(
        lax.broadcasted_iota(jnp.int32, (tok, tok), 0) == lax.broadcasted_iota(jnp.int32, (tok, tok), 1), 1.0, 0.0
    ).astype(BF16)
    ids_rows = dot(ids_ref[...].astype(F32).astype(BF16), eye, 0, 0)
    gate_rows = dot(gate_ref[...], eye, 0, 0)
    ids = [ids_rows[k : k + 1, :] for k in range(2)]
    expert_no = lax.broadcasted_iota(jnp.int32, (NO * NZ // 2, tok), 0).astype(F32)
    hot = [jnp.where(expert_no == ids[k], 1.0, 0.0) for k in range(2)]
    earlier = lax.broadcasted_iota(jnp.int32, (tok, tok), 0) < lax.broadcasted_iota(
        jnp.int32, (tok, tok), 1
    )
    before = dot((hot[0] + hot[1]).astype(BF16), jnp.where(earlier, 1.0, 0.0).astype(BF16))
    code = [
        ids[k] * 16.0 + jnp.sum(before * hot[k], axis=0, keepdims=True) for k in range(2)
    ]
    line = lax.broadcasted_iota(jnp.int32, (8, tok), 0)
    upper = jnp.where(line == 0, code[0], code[1])
    ma[0:8, :] = jnp.where(line < 2, upper, jnp.where(line == 2, gate_rows[0:1, :], gate_rows[1:2, :]))
    pl.semaphore_wait(barrier, len(peers))

    def block(ref, own_ref, j):
        return own_ref if j == 0 else ref.at[(j - 1) * tok : j * tok, :]

    def gather_sent(way, step, n):
        return step < 3 or n == way or (way == 0 and n == 2)

    def gather_copy(way, step, n):
        src = 0 if step == 0 else 2 * step - 1 + way
        dst = 7 if step == 3 else 2 * step + 1 + way
        if n == 2:
            a, b = ma.at[src * 8 : src * 8 + 8, :], ma.at[dst * 8 : dst * 8 + 8, :]
        else:
            ref, own_ref = ((xa, x_ref), (ca, c_ref))[n]
            a, b = block(ref, own_ref, src), block(ref, own_ref, dst)
        sem = (way * 4 + step) * 3 + n
        return remote(a, b, ag_s.at[sem], ag_r.at[sem], {"ep": neighbour[way]})

    def gather_start():
        for n in (2, 0, 1):
            for way in range(2):
                gather_copy(way, 0, n).start()

    def gather_next(step, part):
        for n in ((2, 0), (1,))[part]:
            for way in range(2):
                if gather_sent(way, step, n):
                    gather_copy(way, step, n).wait_recv()
                if step < 3 and gather_sent(way, step + 1, n):
                    gather_copy(way, step + 1, n).start()

    rho = lax.broadcasted_iota(jnp.int32, (BR, tok), 0)
    o_of = rho >> 4
    i_of = rho & 15
    to_yx = ((y + (o_of >> 1)) & (NY - 1)) * NX + ((x + (o_of & 1)) & (NX - 1))
    expert_of = to_yx * (NZ // 2) + z // 2

    def matches(t, j):
        rank = i_of + (TR * t - CAP * j)
        good = jnp.logical_and(rank >= 0, rank < CAP)
        want = jnp.where(good, expert_of * 16 + rank, -1).astype(F32)
        return [want == ma[j * 8 + k : j * 8 + k + 1, :] for k in range(2)]

    def rows_of(t):
        return pl.ds(t * BR, BR)

    def yx_copy(t, part, first, count, o):
        rows = pl.ds(part * slots + t * BR + first, count)
        n = 2 * t + part
        return remote(sx.at[rows, :], rx.at[rows, :], yx_s.at[n], yx_r.at[n], {"ep": at_offset(o, 1)})

    def yx_all(t, part):
        return yx_copy(t, part, TR, BR - TR, 1)

    def select(t, part):
        for n, j in enumerate(SPANS[t]):
            first, second = matches(t, j)
            lanes = pl.ds(n * tok, tok)
            if part == 0:
                smat[rows_of(t), lanes] = jnp.where(jnp.logical_or(first, second), 1.0, 0.0).astype(BF16)
            else:
                gates = [ma[j * 8 + 2 + k : j * 8 + 3 + k, :] for k in range(2)]
                gmat[:, lanes] = jnp.where(first, gates[0], jnp.where(second, gates[1], 0.0)).astype(BF16)
        base = part * slots + t * BR

        def piece(i, carry):
            lanes = pl.ds(pl.multiple_of(i * LC, LC), LC)
            total = None
            for n, j in enumerate(SPANS[t]):
                if part == 0:
                    one = dot(smat[rows_of(t), n * tok : (n + 1) * tok], block(xa, x_ref, j)[:, lanes])
                else:
                    one = dot(gmat[:, n * tok : (n + 1) * tok], block(ca, c_ref, j)[:, lanes])
                total = one if total is None else total + one
            sx[pl.ds(base, BR), lanes] = total.astype(BF16)
            return carry

        lax.fori_loop(0, dl // LC, piece, 0)
        for o in range(1, NO):
            yx_copy(t, part, o * TR, TR, o).start()
        rx[base : base + TR, :] = sx[base : base + TR, :]

    def dp_copy(t, stage):
        sems = (dp_s.at[t * 3 + stage], dp_r.at[t * 3 + stage])
        here = pl.ds(t * half_rows, half_rows)
        if stage == 0:
            return remote(ps.at[here, :], pr.at[here, :], *sems, {"dp": core_peer})
        if stage == 1:
            return remote(qs.at[here, :], qr.at[here, :], *sems, {"dp": hi_peer})
        mine = pl.ds(pl.multiple_of(t * BR + core * half_rows, half_rows), half_rows)
        return remote(ag.at[mine, :], ag.at[mine, :], *sems, {"dp": core_peer})

    def hidden(t):
        yx_all(t, 0).wait_recv()
        yx_all(t, 1).wait_recv()

        def part(i, carry):
            cols = pl.ds(pl.multiple_of(i * LC, LC), LC)
            later = pl.ds(pl.multiple_of(hid + i * LC, LC), LC)
            puf[:, cols] = dot(rx[rows_of(t), :], up_ref[:, cols])
            puf[:, later] = dot(rx[pl.ds(slots + t * BR, BR), :], down_ref[cols, :], 1, 1)
            return carry

        lax.fori_loop(0, hid // LC, part, 0)
        here = pl.ds(t * half_rows, half_rows)
        theirs = pl.ds(pl.multiple_of((1 - core) * half_rows, half_rows), half_rows)
        mine = pl.ds(pl.multiple_of(core * half_rows, half_rows), half_rows)
        ps[here, :] = puf[theirs, :].astype(BF16)
        dp_copy(t, 0).start()
        own[here, :] = puf[mine, :]

    def chip_sum(t):
        dp_copy(t, 0).wait_recv()
        here = pl.ds(t * half_rows, half_rows)
        qs[here, :] = (own[here, :] + pr[here, :].astype(F32)).astype(BF16)
        dp_copy(t, 1).start()

    def activate(t):
        dp_copy(t, 1).wait_recv()
        here = pl.ds(t * half_rows, half_rows)
        mine = pl.ds(pl.multiple_of(t * BR + core * half_rows, half_rows), half_rows)
        preact = qs[here, 0:hid].astype(F32) + qr[here, 0:hid].astype(F32)
        upstream = qs[here, hid : 2 * hid].astype(F32) + qr[here, hid : 2 * hid].astype(F32)
        sig = 1.0 / (1.0 + jnp.exp(-preact))
        act = (preact * sig).astype(BF16)
        ag[mine, 0:hid] = act
        ag[mine, hid : 2 * hid] = (upstream * (sig * (1.0 + preact * (1.0 - sig)))).astype(BF16)
        score = jnp.sum(act.astype(F32) * upstream, axis=1, keepdims=True)
        ag[mine, 2 * hid : 2 * hid + 128] = jnp.broadcast_to(score, (half_rows, 128)).astype(BF16)
        dp_copy(t, 2).start()

    def back_copy(t, o):
        rows = pl.ds(t * BR + o * TR, TR)
        return remote(dxs.at[rows, :], dxr.at[rows, :], rt_s.at[t], rt_r.at[t], {"ep": at_offset(o, -1)})

    def back_all(t):
        rows = pl.ds(t * BR + TR, BR - TR)
        return remote(dxs.at[rows, :], dxr.at[rows, :], rt_s.at[t], rt_r.at[t], {"ep": at_offset(1, -1)})

    def back_rows(t):
        dp_copy(t, 2).wait_recv()

        def part(i, carry):
            cols = pl.ds(pl.multiple_of(i * LC, LC), LC)
            dxs[rows_of(t), cols] = dot(ag[rows_of(t), hid : 2 * hid], up_ref[cols, :], 1, 1).astype(BF16)
            return carry

        lax.fori_loop(0, dl // LC, part, 0)
        dxs[rows_of(t), dl : dl + 128] = ag[rows_of(t), 2 * hid : 2 * hid + 128]

    def send_back(t):
        for o in range(1, NO):
            back_copy(t, o).start()
        dxr[t * BR : t * BR + TR, :] = dxs[t * BR : t * BR + TR, :]

    def token_sum(j, lo, hi_lane):
        total = None
        for t in range(TILES):
            if j in SPANS[t]:
                n = SPANS[t].index(j)
                one = dot(smat[rows_of(t), n * tok : (n + 1) * tok], dxr[rows_of(t), lo:hi_lane], 0, 0)
                total = one if total is None else total + one
        return total

    def score_sum(j):
        sums = [0.0, 0.0]
        for t in range(TILES):
            if j in SPANS[t]:
                value = dxr[rows_of(t), dl : dl + 128].astype(F32)
                for k, hit in enumerate(matches(t, j)):
                    sums[k] = sums[k] + jnp.sum(jnp.where(hit, value, 0.0), axis=0, keepdims=True)
        return jnp.where(line == 0, sums[0], jnp.where(line == 1, sums[1], 0.0))

    def lanes_of(way, m):
        return half_lanes if (way + m) % 2 else 0

    def sum_rows(way, m):
        return slice((way * 7 + m) * tok, (way * 7 + m + 1) * tok)

    def sum_copy(way, m):
        n = way * 7 + m
        rows = pl.ds(n * tok, tok)
        return remote(rso.at[rows, :], rsi.at[rows, :], rs_s.at[n], rs_r.at[n], {"ep": neighbour[way]})

    def score_copy(way, step):
        n = way * 4 + step
        rows = pl.ds(n * 8, 8)
        return remote(sco.at[rows, :], sci.at[rows, :], sc_s.at[n], sc_r.at[n], {"ep": neighbour[way]})

    def scored(way, step):
        return step > 0 or way == 0

    def sum_ready(way, m):
        lo = lanes_of(way, m)
        tf[way * tok : (way + 1) * tok, :] = token_sum(FAR_TO_NEAR[way][(m + 1) // 2], lo, lo + half_lanes)

    def sum_next(way, m):
        total = tf[way * tok : (way + 1) * tok, :]
        if m >= 2:
            sum_copy(way, m - 2).wait_recv()
            total = total + rsi[sum_rows(way, m - 2), :].astype(F32)
        rso[sum_rows(way, m), :] = total.astype(BF16)
        sum_copy(way, m).start()

    def score_next(way, step):
        n = way * 4 + step
        here = score_sum(FAR_TO_NEAR[way][step])
        if step > 0 and scored(way, step - 1):
            score_copy(way, step - 1).wait_recv()
            here = here + sci[n * 8 - 8 : n * 8, :]
        sco[n * 8 : n * 8 + 8, :] = here
        score_copy(way, step).start()

    def up_gradient():
        def part(i, carry):
            cols = pl.ds(pl.multiple_of(i * LC, LC), LC)
            gu_ref[cols, :] = dot(rx[0:slots, cols], ag[:, hid : 2 * hid], 0, 0).astype(BF16)
            return carry

        lax.fori_loop(0, dl // LC, part, 0)

    def down_gradient():
        def part(i, carry):
            cols = pl.ds(pl.multiple_of(i * LC, LC), LC)
            gd_ref[:, cols] = dot(ag[:, 0:hid], rx[slots : 2 * slots, cols], 0, 0).astype(BF16)
            return carry

        lax.fori_loop(0, dl // LC, part, 0)

    gather_start()
    gather_next(0, 0)
    select(0, 0)
    gather_next(0, 1)
    select(0, 1)
    gather_next(1, 0)
    select(1, 0)
    select(2, 0)
    for load in loads:
        load.wait()
    hidden(0)
    chip_sum(0)
    gather_next(1, 1)
    select(1, 1)
    select(2, 1)
    activate(0)
    back_rows(0)
    gather_next(2, 0)
    select(3, 0)
    hidden(1)
    chip_sum(1)
    gather_next(2, 1)
    select(3, 1)
    activate(1)
    hidden(2)
    chip_sum(2)
    gather_next(3, 0)
    select(4, 0)
    gather_next(3, 1)
    select(4, 1)
    back_rows(1)
    activate(2)
    back_rows(2)
    hidden(3)
    chip_sum(3)
    hidden(4)
    chip_sum(4)
    activate(3)
    activate(4)
    back_rows(4)
    send_back(4)
    back_rows(3)
    send_back(3)
    send_back(2)
    send_back(1)
    send_back(0)
    stores = [
        pltpu.make_async_copy(gu_ref, gu_hbm, w_s.at[2]),
        pltpu.make_async_copy(gd_ref, gd_hbm, w_s.at[3]),
    ]
    up_gradient()
    stores[0].start()
    back_all(4).wait_recv()
    for way in range(2):
        sum_ready(way, 0)
        sum_next(way, 0)
    back_all(3).wait_recv()
    for m in range(1, 7):
        if m == 3:
            back_all(2).wait_recv()
            back_all(1).wait_recv()
        if m == 5:
            back_all(0).wait_recv()
        for way in range(2):
            sum_ready(way, m)
            sum_next(way, m)
        if m == 1:
            down_gradient()
            stores[1].start()
        if m % 2 == 0:
            for way in range(2):
                if m == 2 and way == 0:
                    score_next(0, 0)
                score_next(way, m // 2)
    for n, lo in enumerate((0, half_lanes)):
        tf[n * tok : (n + 1) * tok, :] = token_sum(0, lo, lo + half_lanes)
    scores = score_sum(0)
    for m in (5, 6):
        for way in range(2):
            sum_copy(way, m).wait_recv()
    for m in (5, 6):
        lo = lanes_of(0, m)
        n = lo // half_lanes
        gx_ref[:, lo : lo + half_lanes] = (
            tf[n * tok : (n + 1) * tok, :]
            + rsi[sum_rows(0, m), :].astype(F32)
            + rsi[sum_rows(1, 11 - m), :].astype(F32)
        ).astype(BF16)
    for way in range(2):
        score_copy(way, 3).wait_recv()
    gates = jnp.where(line == 0, ma[2:3, :], jnp.where(line == 1, ma[3:4, :], 1.0))
    gs_ref[...] = (scores + sci[24:32, :] + sci[56:64, :]) / gates

    for way in range(2):
        for step in range(4):
            for n in range(3):
                if gather_sent(way, step, n):
                    gather_copy(way, step, n).wait_send()
            if scored(way, step):
                score_copy(way, step).wait_send()
        for m in range(7):
            sum_copy(way, m).wait_send()
    for t in range(TILES):
        for part in range(2):
            yx_all(t, part).wait_send()
        back_all(t).wait_send()
        for stage in range(3):
            dp_copy(t, stage).wait_send()
    for store in stores:
        store.wait()


def on_device(tokens, cotangent, gate_prob, expert_ids, w_up, w_down):
    tok, dl = tokens.shape
    hid = w_up.shape[2]
    vmem = pl.BlockSpec(memory_space=pltpu.VMEM)
    hbm = pl.BlockSpec(memory_space=pl.ANY)
    rows = TILES * BR
    halves = rows // 2
    wide = max(len(s) for s in SPANS) * tok
    scratch = [
        pltpu.VMEM((7 * tok, dl), BF16),
        pltpu.VMEM((7 * tok, dl), BF16),
        pltpu.VMEM((8 * 8, tok), F32),
        pltpu.VMEM((rows, wide), BF16),
        pltpu.VMEM((BR, wide), BF16),
        pltpu.VMEM((2 * rows, dl), BF16),
        pltpu.VMEM((2 * rows, dl), BF16),
        pltpu.VMEM((BR, 2 * hid), F32),
        pltpu.VMEM((halves, 2 * hid), F32),
        pltpu.VMEM((halves, 2 * hid), BF16),
        pltpu.VMEM((halves, 2 * hid), BF16),
        pltpu.VMEM((halves, 2 * hid), BF16),
        pltpu.VMEM((halves, 2 * hid), BF16),
        pltpu.VMEM((rows, 2 * hid + 128), BF16),
        pltpu.VMEM((rows, dl + 128), BF16),
        pltpu.VMEM((rows, dl + 128), BF16),
        pltpu.VMEM((14 * tok, dl // 2), BF16),
        pltpu.VMEM((14 * tok, dl // 2), BF16),
        pltpu.VMEM((8 * 8, tok), F32),
        pltpu.VMEM((8 * 8, tok), F32),
        pltpu.VMEM((2 * tok, dl // 2), F32),
        pltpu.VMEM((dl, hid), BF16),
        pltpu.VMEM((hid, dl), BF16),
        pltpu.VMEM((dl, hid), BF16),
        pltpu.VMEM((hid, dl), BF16),
        pltpu.SemaphoreType.DMA((4,)),
    ]
    for count in (24, 2 * TILES, 3 * TILES, TILES, 14, 8):
        scratch += [pltpu.SemaphoreType.DMA((count,))] * 2
    grad_tokens, scores, grad_up, grad_down = pl.pallas_call(
        kernel,
        out_shape=(
            jax.ShapeDtypeStruct((tok, dl), BF16),
            jax.ShapeDtypeStruct((8, tok), F32),
            jax.ShapeDtypeStruct((dl, hid), BF16),
            jax.ShapeDtypeStruct((hid, dl), BF16),
        ),
        in_specs=[vmem] * 4 + [hbm] * 2,
        out_specs=(vmem, vmem, hbm, hbm),
        scratch_shapes=scratch,
        compiler_params=pltpu.CompilerParams(
            collective_id=0, has_side_effects=True, vmem_limit_bytes=60 * 2**20
        ),
    )(tokens, cotangent, gate_prob, expert_ids, w_up[0], w_down[0])
    return grad_tokens, scores[:2].T, grad_up[None], grad_down[None]


def solution(mesh):
    in_specs = (
        P("ep", "dp"),
        P("ep", "dp"),
        P("ep", None),
        P("ep", None),
        P("ep", "dp", None),
        P("ep", None, "dp"),
    )
    out_specs = (P("ep", "dp"), P("ep", None), P("ep", "dp", None), P("ep", None, "dp"))
    return jax.shard_map(
        on_device, mesh=mesh, in_specs=in_specs, out_specs=out_specs, check_vma=False
    )
```

time: 197 us -> 165 us (0.84)
  Pallas kernels: 187 us -> 154 us
  local copies, waits for them, and re-layouts: 7.34 us -> 10.1 us
  other arithmetic: 2 us -> 0 us
    pallas_call x1, Pallas kernels: 187 us -> 154 us  [on_device(): pl.pallas_call(kernel, out_shape=(jax.ShapeDtypeStruct((tok, dl), BF16),...]
    unnamed x5 -> x7, local copies, waits for them, and re-layouts: 6.03 us -> 8.82 us
where the time goes in v2:
time: 165 us
  Pallas kernels  154 us (93%)
  local copies, waits for them, and re-layouts  10.1 us (6%)
    pallas_call x1, Pallas kernels, on_device(): pl.pallas_call(kernel, out_shape=(jax.ShapeDtypeStruct((tok, dl), BF16),...  154 us
    unnamed x7, local copies, waits for them, and re-layouts  8.82 us

profile of v2, /device:TPU:2, one launch (start us, length us, event | category | flops | bytes accessed | tf_op | source)
XLA Modules:
  0.0 165.0 jit_solution(1617025190834384726)
XLA Ops:
  0.6 1.4 copy.10.gate_ref
  2.0 1.4 copy.11.ids_ref
  3.4 154.3 %shard_map.93 = (bf16[128,1792]{1,0:T(8,128)(2,1)}, f32[8,128]{1,0:T(8,128)}, bf16[1792,512]{1,0:T(8,128)(2,1)}, bf16[512,1792]{1,0:T(8,128)(2,1)}) custom-call(bf16[128,1792]{1,0:T(8,128)(2,1)} %x_ref.1, bf16[128,1792]{1,0:T(8,128)(2,1)} %c_ref.1, bf16[128,2]{1,0:T(8,128)(2,1)} %copy.10.gate_ref, s32[128,2]{1,0:T(8,128)} %copy.11.ids_ref, ...), custom_call_target="tpu_custom_call" | custom-call | tf_op jit(solution)/shard_map/pallas_call | solution.py:472
  157.8 1.2 slice_bitcast_fusion
  159.0 1.8 %copy.15 = bf16[128,1792]{1,0:T(8,128)(2,1)} copy(bf16[128,1792]{1,0:T(8,128)(2,1)} %get-tuple-element.16) | data formatting | bytes 917504
  160.8 0.0 copy-start
  160.8 3.0 %copy.16 = bf16[1,1792,512]{2,1,0:T(8,128)(2,1)} copy(bf16[1,1792,512]{2,1,0:T(8,128)(2,1)} %bitcast.9) | data formatting | bytes 3670016
  163.8 0.0 copy-done
  163.8 1.2 copy.17
Async XLA Ops:
  160.8 3.0 %copy-start = (bf16[512,1792]{1,0:T(8,128)(2,1)S(1)}, bf16[512,1792]{1,0:T(8,128)(2,1)}, u32[]{:S(2)}) copy-start(bf16[512,1792]{1,0:T(8,128)(2,1)} %get-tuple-element.11) | copy-start | bytes 5505028

commit v3 on v2

--- a/solution.py
+++ b/solution.py
@@ -15,12 +15,14 @@
 TR = 16
 TILES = NZ * CAP // TR
 BR = NO * TR
+LAST = NO * CAP
 DISP = (0, -1, 1, -2, 2, -3, 3, 4)
 SPANS = tuple(
     tuple(sorted({(TR * t + i) // CAP for i in range(TR)})) for t in range(TILES)
 )
 FAR_TO_NEAR = ((7, 6, 4, 2), (7, 5, 3, 1))
 LC = 256
+PIECES = 4
 
 
 def dot(a, b, ca=1, cb=0):
@@ -31,7 +33,8 @@
     x_ref, c_ref, gate_ref, ids_ref, up_hbm, down_hbm,
     gx_ref, gs_ref, gu_hbm, gd_hbm,
     xa, ca, ma, smat, gmat, sx, rx, puf, own, ps, pr, qs, qr, ag, dxs, dxr,
-    rso, rsi, sco, sci, tf, up_ref, down_ref, gu_ref, gd_ref, w_s,
+    rso, rsi, sco, sci, tf, up_ref, down_ref, gu_ref, gd_ref, lmat, lgate, lout, lin, pm, w_s,
+    last_s, last_r,
     ag_s, ag_r, yx_s, yx_r, dp_s, dp_r, rt_s, rt_r, rs_s, rs_r, sc_s, sc_r,
 ):
     tok, dl = x_ref.shape
@@ -71,11 +74,8 @@
     for load in loads:
         load.start()
 
-    eye = jnp.where(
-        lax.broadcasted_iota(jnp.int32, (tok, tok), 0) == lax.broadcasted_iota(jnp.int32, (tok, tok), 1), 1.0, 0.0
-    ).astype(BF16)
-    ids_rows = dot(ids_ref[...].astype(F32).astype(BF16), eye, 0, 0)
-    gate_rows = dot(gate_ref[...], eye, 0, 0)
+    gate_rows = gate_ref[...].astype(F32)
+    ids_rows = ids_ref[...].astype(F32)
     ids = [ids_rows[k : k + 1, :] for k in range(2)]
     expert_no = lax.broadcasted_iota(jnp.int32, (NO * NZ // 2, tok), 0).astype(F32)
     hot = [jnp.where(expert_no == ids[k], 1.0, 0.0) for k in range(2)]
@@ -95,7 +95,7 @@
         return own_ref if j == 0 else ref.at[(j - 1) * tok : j * tok, :]
 
     def gather_sent(way, step, n):
-        return step < 3 or n == way or (way == 0 and n == 2)
+        return step < 3 or (way == 0 and n == 2)
 
     def gather_copy(way, step, n):
         src = 0 if step == 0 else 2 * step - 1 + way
@@ -115,11 +115,46 @@
 
     def gather_next(step, part):
         for n in ((2, 0), (1,))[part]:
-            for way in range(2):
+            for way in (part, 1 - part):
                 if gather_sent(way, step, n):
                     gather_copy(way, step, n).wait_recv()
                 if step < 3 and gather_sent(way, step + 1, n):
                     gather_copy(way, step + 1, n).start()
+                if step == 2 and n == way:
+                    last_hop(way)
+
+    def last_copy(way, h):
+        n = way * 2 + h
+        rows, lanes = pl.ds(way * LAST, LAST), pl.ds(h * half_lanes, half_lanes)
+        return remote(
+            lout.at[rows, lanes], lin.at[rows, lanes], last_s.at[n], last_r.at[n], {"ep": neighbour[way]}
+        )
+
+    def last_hop(way):
+        j = 5 + way
+        spot = lax.broadcasted_iota(jnp.int32, (LAST, tok), 0)
+        o_at = (spot * 205) >> 11
+        there = ((y + (o_at >> 1)) & (NY - 1)) * NX + ((x + (o_at & 1)) & (NX - 1))
+        pair = ((z + (1, NZ - 1)[way]) % NZ) // 2
+        want = ((there * (NZ // 2) + pair) * 16 + (spot - o_at * CAP)).astype(F32)
+        first, second = [want == ma[j * 8 + k : j * 8 + k + 1, :] for k in range(2)]
+        mine = slice(way * LAST, (way + 1) * LAST)
+        lmat[mine, :] = jnp.where(jnp.logical_or(first, second), 1.0, 0.0).astype(BF16)
+        if way == 1:
+            gates = [ma[j * 8 + 2 + k : j * 8 + 3 + k, :] for k in range(2)]
+            lgate[...] = jnp.where(first, gates[0], jnp.where(second, gates[1], 0.0)).astype(BF16)
+        ref, own_ref = ((xa, x_ref), (ca, c_ref))[way]
+
+        def piece(i, carry):
+            lanes = pl.ds(pl.multiple_of(i * 128, 128), 128)
+            pick = lmat[mine, :] if way == 0 else lgate[...]
+            lout[mine, lanes] = dot(pick, block(ref, own_ref, j)[:, lanes]).astype(BF16)
+            return carry
+
+        each = half_lanes // 128
+        for h in range(2):
+            lax.fori_loop(h * each, (h + 1) * each, piece, 0)
+            last_copy(way, h).start()
 
     rho = lax.broadcasted_iota(jnp.int32, (BR, tok), 0)
     o_of = rho >> 4
@@ -136,30 +171,44 @@
     def rows_of(t):
         return pl.ds(t * BR, BR)
 
-    def yx_copy(t, part, first, count, o):
+    def yx_copy(t, part, h, first, count, o):
         rows = pl.ds(part * slots + t * BR + first, count)
+        lanes = pl.ds(0, dl)
         n = 2 * t + part
-        return remote(sx.at[rows, :], rx.at[rows, :], yx_s.at[n], yx_r.at[n], {"ep": at_offset(o, 1)})
+        if t == TILES - 1:
+            lanes = pl.ds(h * half_lanes, half_lanes)
+            n += part + h
+        return remote(
+            sx.at[rows, lanes], rx.at[rows, lanes], yx_s.at[n], yx_r.at[n], {"ep": at_offset(o, 1)}
+        )
 
     def yx_all(t, part):
-        return yx_copy(t, part, TR, BR - TR, 1)
-
-    def select(t, part):
+        return [yx_copy(t, part, h, TR, BR - TR, 1) for h in range(2 if t == TILES - 1 else 1)]
+
+    def pick_matrices(t, part):
         for n, j in enumerate(SPANS[t]):
             first, second = matches(t, j)
             lanes = pl.ds(n * tok, tok)
             if part == 0:
                 smat[rows_of(t), lanes] = jnp.where(jnp.logical_or(first, second), 1.0, 0.0).astype(BF16)
-            else:
+            elif j < 7:
                 gates = [ma[j * 8 + 2 + k : j * 8 + 3 + k, :] for k in range(2)]
                 gmat[:, lanes] = jnp.where(first, gates[0], jnp.where(second, gates[1], 0.0)).astype(BF16)
+
+    def select(t, part, h=0):
+        if h == 0:
+            pick_matrices(t, part)
         base = part * slots + t * BR
+        last = t == TILES - 1
+        width = 128 if last else LC
 
         def piece(i, carry):
-            lanes = pl.ds(pl.multiple_of(i * LC, LC), LC)
+            lanes = pl.ds(pl.multiple_of(i * width, width), width)
             total = None
             for n, j in enumerate(SPANS[t]):
-                if part == 0:
+                if j == 7:
+                    one = dot(pm[...], lin[part * LAST : (part + 1) * LAST, lanes])
+                elif part == 0:
                     one = dot(smat[rows_of(t), n * tok : (n + 1) * tok], block(xa, x_ref, j)[:, lanes])
                 else:
                     one = dot(gmat[:, n * tok : (n + 1) * tok], block(ca, c_ref, j)[:, lanes])
@@ -167,10 +216,12 @@
             sx[pl.ds(base, BR), lanes] = total.astype(BF16)
             return carry
 
-        lax.fori_loop(0, dl // LC, piece, 0)
+        each = half_lanes // 128
+        lax.fori_loop(*((h * each, (h + 1) * each) if last else (0, dl // LC)), piece, 0)
         for o in range(1, NO):
-            yx_copy(t, part, o * TR, TR, o).start()
-        rx[base : base + TR, :] = sx[base : base + TR, :]
+            yx_copy(t, part, h, o * TR, TR, o).start()
+        span = slice(h * half_lanes, (h + 1) * half_lanes) if last else slice(0, dl)
+        rx[base : base + TR, span] = sx[base : base + TR, span]
 
     def dp_copy(t, stage):
         sems = (dp_s.at[t * 3 + stage], dp_r.at[t * 3 + stage])
@@ -183,8 +234,9 @@
         return remote(ag.at[mine, :], ag.at[mine, :], *sems, {"dp": core_peer})
 
     def hidden(t):
-        yx_all(t, 0).wait_recv()
-        yx_all(t, 1).wait_recv()
+        for half in range(2):
+            for copy in yx_all(t, half):
+                copy.wait_recv()
 
         def part(i, carry):
             cols = pl.ds(pl.multiple_of(i * LC, LC), LC)
@@ -271,7 +323,7 @@
 
     def sum_copy(way, m):
         n = way * 7 + m
-        rows = pl.ds(n * tok, tok)
+        rows = pl.ds(n * tok, tok if m else LAST)
         return remote(rso.at[rows, :], rsi.at[rows, :], rs_s.at[n], rs_r.at[n], {"ep": neighbour[way]})
 
     def score_copy(way, step):
@@ -284,14 +336,25 @@
 
     def sum_ready(way, m):
         lo = lanes_of(way, m)
+        if m == 0:
+            tf[way * tok : way * tok + LAST, :] = dot(
+                pm[...], dxr[rows_of(TILES - 1), lo : lo + half_lanes], 0, 0
+            )
+            return
         tf[way * tok : (way + 1) * tok, :] = token_sum(FAR_TO_NEAR[way][(m + 1) // 2], lo, lo + half_lanes)
 
     def sum_next(way, m):
-        total = tf[way * tok : (way + 1) * tok, :]
+        count = tok if m else LAST
+        total = tf[way * tok : way * tok + count, :]
+        first = (way * 7 + m) * tok
         if m >= 2:
             sum_copy(way, m - 2).wait_recv()
+        if m == 2:
+            came = rsi[first - 2 * tok : first - 2 * tok + LAST, :]
+            total = total + dot(lmat[(1 - way) * LAST : (2 - way) * LAST, :], came, 0, 0)
+        elif m > 2:
             total = total + rsi[sum_rows(way, m - 2), :].astype(F32)
-        rso[sum_rows(way, m), :] = total.astype(BF16)
+        rso[first : first + count, :] = total.astype(BF16)
         sum_copy(way, m).start()
 
     def score_next(way, step):
@@ -327,6 +390,10 @@
     gather_next(1, 0)
     select(1, 0)
     select(2, 0)
+    slot_row = lax.broadcasted_iota(jnp.int32, (BR, LAST), 0)
+    rank_row = (slot_row & 15) - (TR - CAP)
+    spot_of = jnp.where(rank_row >= 0, (slot_row >> 4) * CAP + rank_row, -1)
+    pm[...] = jnp.where(spot_of == lax.broadcasted_iota(jnp.int32, (BR, LAST), 1), 1.0, 0.0).astype(BF16)
     for load in loads:
         load.wait()
     hidden(0)
@@ -345,10 +412,11 @@
     activate(1)
     hidden(2)
     chip_sum(2)
-    gather_next(3, 0)
-    select(4, 0)
-    gather_next(3, 1)
-    select(4, 1)
+    gather_copy(0, 3, 2).wait_recv()
+    for h in range(2):
+        for part in range(2):
+            last_copy(part, h).wait_recv()
+            select(4, part, h)
     back_rows(1)
     activate(2)
     back_rows(2)
@@ -410,7 +478,7 @@
     for way in range(2):
         score_copy(way, 3).wait_recv()
     gates = jnp.where(line == 0, ma[2:3, :], jnp.where(line == 1, ma[3:4, :], 1.0))
-    gs_ref[...] = (scores + sci[24:32, :] + sci[56:64, :]) / gates
+    gs_ref[...] = ((scores + sci[24:32, :] + sci[56:64, :]) / gates)[0:2, :]
 
     for way in range(2):
         for step in range(4):
@@ -421,12 +489,35 @@
                 score_copy(way, step).wait_send()
         for m in range(7):
             sum_copy(way, m).wait_send()
+        for h in range(2):
+            last_copy(way, h).wait_send()
     for t in range(TILES):
         for part in range(2):
-            yx_all(t, part).wait_send()
+            for copy in yx_all(t, part):
+                copy.wait_send()
         back_all(t).wait_send()
         for stage in range(3):
             dp_copy(t, stage).wait_send()
+    for store in stores:
+        store.wait()
+
+
+def hand_over(*refs):
+    sems = refs[12]
+    loads, stores = [], []
+    for n in range(4):
+        pieces = PIECES if refs[n].shape[0] % (16 * PIECES) == 0 else 1
+        size = refs[n].shape[0] // pieces
+        for i in range(pieces):
+            rows = pl.ds(i * size, size)
+            held = refs[8 + n].at[rows, :]
+            loads.append(pltpu.make_async_copy(refs[n].at[rows, :], held, sems.at[0, n, i]))
+            stores.append(pltpu.make_async_copy(held, refs[4 + n].at[rows, :], sems.at[1, n, i]))
+    for load in loads:
+        load.start()
+    for load, store in zip(loads, stores):
+        load.wait()
+        store.start()
     for store in stores:
         store.wait()
 
@@ -440,8 +531,8 @@
     halves = rows // 2
     wide = max(len(s) for s in SPANS) * tok
     scratch = [
-        pltpu.VMEM((7 * tok, dl), BF16),
-        pltpu.VMEM((7 * tok, dl), BF16),
+        pltpu.VMEM((6 * tok, dl), BF16),
+        pltpu.VMEM((6 * tok, dl), BF16),
         pltpu.VMEM((8 * 8, tok), F32),
         pltpu.VMEM((rows, wide), BF16),
         pltpu.VMEM((BR, wide), BF16),
@@ -465,15 +556,24 @@
         pltpu.VMEM((hid, dl), BF16),
         pltpu.VMEM((dl, hid), BF16),
         pltpu.VMEM((hid, dl), BF16),
+        pltpu.VMEM((2 * LAST, tok), BF16),
+        pltpu.VMEM((LAST, tok), BF16),
+        pltpu.VMEM((2 * LAST, dl), BF16),
+        pltpu.VMEM((2 * LAST, dl), BF16),
+        pltpu.VMEM((BR, LAST), BF16),
+    ]
+    scratch += [
+        pltpu.SemaphoreType.DMA((4,)),
+        pltpu.SemaphoreType.DMA((4,)),
         pltpu.SemaphoreType.DMA((4,)),
     ]
-    for count in (24, 2 * TILES, 3 * TILES, TILES, 14, 8):
+    for count in (24, 2 * TILES + 2, 3 * TILES, TILES, 14, 8):
         scratch += [pltpu.SemaphoreType.DMA((count,))] * 2
     grad_tokens, scores, grad_up, grad_down = pl.pallas_call(
         kernel,
         out_shape=(
             jax.ShapeDtypeStruct((tok, dl), BF16),
-            jax.ShapeDtypeStruct((8, tok), F32),
+            jax.ShapeDtypeStruct((2, tok), F32),
             jax.ShapeDtypeStruct((dl, hid), BF16),
             jax.ShapeDtypeStruct((hid, dl), BF16),
         ),
@@ -483,8 +583,16 @@
         compiler_params=pltpu.CompilerParams(
             collective_id=0, has_side_effects=True, vmem_limit_bytes=60 * 2**20
         ),
-    )(tokens, cotangent, gate_prob, expert_ids, w_up[0], w_down[0])
-    return grad_tokens, scores[:2].T, grad_up[None], grad_down[None]
+    )(tokens, cotangent, gate_prob.T, expert_ids.T, w_up[0], w_down[0])
+    made = (grad_tokens, scores, grad_up, grad_down)
+    grad_tokens, scores, grad_up, grad_down = pl.pallas_call(
+        hand_over,
+        out_shape=tuple(jax.ShapeDtypeStruct(a.shape, a.dtype) for a in made),
+        in_specs=[hbm] * 4,
+        out_specs=(hbm,) * 4,
+        scratch_shapes=[pltpu.VMEM(a.shape, a.dtype) for a in made] + [pltpu.SemaphoreType.DMA((2, 4, PIECES))],
+    )(*made)
+    return grad_tokens, scores.T, grad_up[None], grad_down[None]
 
 
 def solution(mesh):

time: 165 us -> 160 us (0.970)
  local copies, waits for them, and re-layouts: 10.1 us -> 0 us
  Pallas kernels: 154 us -> 159 us
    unnamed x7 -> x0, local copies, waits for them, and re-layouts: 8.82 us -> none
    pallas_call x0 -> x1, Pallas kernels: none -> 4.01 us  [on_device(): pl.pallas_call(hand_over, out_shape=tuple((jax.ShapeDtypeStruct(a.shape,...]
where the time goes in v3:
time: 160 us
  Pallas kernels  159 us (99%)
    pallas_call x1, Pallas kernels, on_device(): pl.pallas_call(kernel, out_shape=(jax.ShapeDtypeStruct((tok, dl), BF16),...  155 us
    pallas_call x1, Pallas kernels, on_device(): pl.pallas_call(hand_over, out_shape=tuple((jax.ShapeDtypeStruct(a.shape,...  4.01 us

profile of v3, /device:TPU:2, one launch (start us, length us, event | category | flops | bytes accessed | tf_op | source)
XLA Modules:
  0.0 159.8 jit_solution(15667535410163538939)
XLA Ops:
  0.6 155.1 %shard_map.93 = (bf16[128,1792]{1,0:T(8,128)(2,1)}, f32[2,128]{1,0:T(2,128)}, bf16[1792,512]{1,0:T(8,128)(2,1)}, bf16[512,1792]{1,0:T(8,128)(2,1)}) custom-call(bf16[128,1792]{1,0:T(8,128)(2,1)} %x_ref.1, bf16[128,1792]{1,0:T(8,128)(2,1)} %c_ref.1, bf16[2,128]{1,0:T(2,128)(2,1)} %bitcast.10, s32[2,128]{1,0:T(2,128)} %bitcast.9, bf16[1792,512]{1,0:T(8,128)(2,1)} %bitcast.7, ...), custom_call_target="tpu_custom_call" | custom-call | tf_op jit(solution)/shard_map/pallas_call | solution.py:572
  155.8 4.0 %shard_map.94 = (bf16[128,1792]{1,0:T(8,128)(2,1)}, f32[2,128]{1,0:T(2,128)}, bf16[1792,512]{1,0:T(8,128)(2,1)}, bf16[512,1792]{1,0:T(8,128)(2,1)}) custom-call(bf16[128,1792]{1,0:T(8,128)(2,1)} %get-tuple-element.12.refs_0_, f32[2,128]{1,0:T(2,128)} %get-tuple-element.13.refs_1_, bf16[1792,512]{1,0:T(8,128)(2,1)} %get-tuple-element.14.refs_2_, ...), custom_call_target="tpu_custom_call" | custom-call | tf_op jit(solution)/shard_map/pallas_call | solution.py:588

commit v4 on v3

--- a/solution.py
+++ b/solution.py
@@ -417,20 +417,20 @@
         for part in range(2):
             last_copy(part, h).wait_recv()
             select(4, part, h)
-    back_rows(1)
-    activate(2)
-    back_rows(2)
     hidden(3)
     chip_sum(3)
     hidden(4)
     chip_sum(4)
+    activate(2)
     activate(3)
+    back_rows(3)
     activate(4)
+    send_back(3)
     back_rows(4)
     send_back(4)
-    back_rows(3)
-    send_back(3)
+    back_rows(2)
     send_back(2)
+    back_rows(1)
     send_back(1)
     send_back(0)
     stores = [
@@ -447,10 +447,11 @@
     for m in range(1, 7):
         if m == 3:
             back_all(2).wait_recv()
-            back_all(1).wait_recv()
-        if m == 5:
-            back_all(0).wait_recv()
         for way in range(2):
+            if (way, m) == (1, 3):
+                back_all(1).wait_recv()
+            if (way, m) == (1, 5):
+                back_all(0).wait_recv()
             sum_ready(way, m)
             sum_next(way, m)
         if m == 1:

time: 160 us -> 159 us (level)
  no operation moved by 1% of the time
where the time goes in v4:
time: 159 us
  Pallas kernels  159 us (100%)
    pallas_call x1, Pallas kernels, on_device(): pl.pallas_call(kernel, out_shape=(jax.ShapeDtypeStruct((tok, dl), BF16),...  155 us
    pallas_call x1, Pallas kernels, on_device(): pl.pallas_call(hand_over, out_shape=tuple((jax.ShapeDtypeStruct(a.shape,...  4.01 us

profile of v4, /device:TPU:2, one launch (start us, length us, event | category | flops | bytes accessed | tf_op | source)
XLA Modules:
  0.0 159.2 jit_solution(2436048870002883093)
XLA Ops:
  0.6 154.5 %shard_map.93 = (bf16[128,1792]{1,0:T(8,128)(2,1)}, f32[2,128]{1,0:T(2,128)}, bf16[1792,512]{1,0:T(8,128)(2,1)}, bf16[512,1792]{1,0:T(8,128)(2,1)}) custom-call(bf16[128,1792]{1,0:T(8,128)(2,1)} %x_ref.1, bf16[128,1792]{1,0:T(8,128)(2,1)} %c_ref.1, bf16[2,128]{1,0:T(2,128)(2,1)} %bitcast.10, s32[2,128]{1,0:T(2,128)} %bitcast.9, bf16[1792,512]{1,0:T(8,128)(2,1)} %bitcast.7, ...), custom_call_target="tpu_custom_call" | custom-call | tf_op jit(solution)/shard_map/pallas_call | solution.py:573
  155.2 4.0 %shard_map.94 = (bf16[128,1792]{1,0:T(8,128)(2,1)}, f32[2,128]{1,0:T(2,128)}, bf16[1792,512]{1,0:T(8,128)(2,1)}, bf16[512,1792]{1,0:T(8,128)(2,1)}) custom-call(bf16[128,1792]{1,0:T(8,128)(2,1)} %get-tuple-element.12.refs_0_, f32[2,128]{1,0:T(2,128)} %get-tuple-element.13.refs_1_, bf16[1792,512]{1,0:T(8,128)(2,1)} %get-tuple-element.14.refs_2_, ...), custom_call_target="tpu_custom_call" | custom-call | tf_op jit(solution)/shard_map/pallas_call | solution.py:589

commit v5 on v4

--- a/solution.py
+++ b/solution.py
@@ -374,13 +374,13 @@
 
         lax.fori_loop(0, dl // LC, part, 0)
 
-    def down_gradient():
+    def down_gradient(first, last):
         def part(i, carry):
             cols = pl.ds(pl.multiple_of(i * LC, LC), LC)
             gd_ref[:, cols] = dot(ag[:, 0:hid], rx[slots : 2 * slots, cols], 0, 0).astype(BF16)
             return carry
 
-        lax.fori_loop(0, dl // LC, part, 0)
+        lax.fori_loop(first, last, part, 0)
 
     gather_start()
     gather_next(0, 0)
@@ -455,7 +455,11 @@
             sum_ready(way, m)
             sum_next(way, m)
         if m == 1:
-            down_gradient()
+            down_gradient(0, 3)
+        if m == 3:
+            down_gradient(3, 5)
+        if m == 4:
+            down_gradient(5, dl // LC)
             stores[1].start()
         if m % 2 == 0:
             for way in range(2):

time: 159 us -> 159 us (level)
  no operation moved by 1% of the time
where the time goes in v5:
time: 159 us
  Pallas kernels  159 us (100%)
    pallas_call x1, Pallas kernels, on_device(): pl.pallas_call(kernel, out_shape=(jax.ShapeDtypeStruct((tok, dl), BF16),...  154 us
    pallas_call x1, Pallas kernels, on_device(): pl.pallas_call(hand_over, out_shape=tuple((jax.ShapeDtypeStruct(a.shape,...  4.01 us

profile of v5, /device:TPU:2, one launch (start us, length us, event | category | flops | bytes accessed | tf_op | source)
XLA Modules:
  0.0 159.1 jit_solution(13867461477047304514)
XLA Ops:
  0.6 154.5 %shard_map.93 = (bf16[128,1792]{1,0:T(8,128)(2,1)}, f32[2,128]{1,0:T(2,128)}, bf16[1792,512]{1,0:T(8,128)(2,1)}, bf16[512,1792]{1,0:T(8,128)(2,1)}) custom-call(bf16[128,1792]{1,0:T(8,128)(2,1)} %x_ref.1, bf16[128,1792]{1,0:T(8,128)(2,1)} %c_ref.1, bf16[2,128]{1,0:T(2,128)(2,1)} %bitcast.10, s32[2,128]{1,0:T(2,128)} %bitcast.9, bf16[1792,512]{1,0:T(8,128)(2,1)} %bitcast.7, ...), custom_call_target="tpu_custom_call" | custom-call | tf_op jit(solution)/shard_map/pallas_call | solution.py:577
  155.1 4.0 %shard_map.94 = (bf16[128,1792]{1,0:T(8,128)(2,1)}, f32[2,128]{1,0:T(2,128)}, bf16[1792,512]{1,0:T(8,128)(2,1)}, bf16[512,1792]{1,0:T(8,128)(2,1)}) custom-call(bf16[128,1792]{1,0:T(8,128)(2,1)} %get-tuple-element.12.refs_0_, f32[2,128]{1,0:T(2,128)} %get-tuple-element.13.refs_1_, bf16[1792,512]{1,0:T(8,128)(2,1)} %get-tuple-element.14.refs_2_, ...), custom_call_target="tpu_custom_call" | custom-call | tf_op jit(solution)/shard_map/pallas_call | solution.py:593
